TPU v7x, 512 devices: a whole 4x4x16 slice. The times are simulated.
512 devices in a mesh: seg: 32 (over z_lo, y, core), dev: 16 (over z_hi, x).
Axes of the slice: x: 4, y: 4, z: 16 (z_hi: 4, z_lo: 4; z = z_hi * 4 + z_lo), core: 2. Of those that a mesh axis runs over, the one named last changes fastest.
Arguments:
- queries: bfloat16 [65536, 1536], P(('seg', 'dev')), may hold values from -12 to 12
- keys: bfloat16 [65536, 1536], P(('seg', 'dev')), may hold values from -12 to 12
- values: bfloat16 [65536, 1536], P(('seg', 'dev')), may hold values from -4 to 4
Outputs:
- grad_queries: bfloat16 [65536, 1536], P(('seg', 'dev'))
- grad_keys: bfloat16 [65536, 1536], P(('seg', 'dev'))
- grad_values: bfloat16 [65536, 1536], P(('seg', 'dev'))
All inputs are finite; a program needn't handle non-finite values.
Results may differ from a plain program's by a relative error of at most 0.015.
Values may be sent and summed in bfloat16 or wider, within the bound.
A program may use at most 128 MiB of HBM per device.

v0:
```python
import jax
import jax.numpy as jnp
from jax import lax
from jax.sharding import PartitionSpec as P

HEADS = 16
WINDOW = 256


def passed_along(value, axis, steps):
    count = lax.axis_size(axis)
    initial, last = (max(0, -steps), min(count, count - steps))
    return lax.ppermute(value, axis, [(source, source + steps) for source in range(initial, last)])


def student_pass(block_q, ext_keys, ext_values, target, first_row, head_count):
    row_count, model_width = block_q.shape
    ext_count = ext_keys.shape[0]
    reach_rows = ext_count - row_count
    head_dim = model_width // head_count
    factor = head_dim ** (-0.5)
    query_heads = block_q.reshape(row_count, head_count, head_dim)
    key_heads = ext_keys.reshape(ext_count, head_count, head_dim)
    value_heads = ext_values.reshape(ext_count, head_count, head_dim)
    scores = (
        jnp.einsum("fhd,ehd->hfe", query_heads, key_heads, preferred_element_type=jnp.float32)
        * factor
    )
    query_pos = first_row + lax.iota(jnp.int32, row_count)
    key_pos = first_row - reach_rows + lax.iota(jnp.int32, ext_count)
    allowed = (
        (key_pos[None, :] <= query_pos[:, None])
        & (key_pos[None, :] >= query_pos[:, None] - reach_rows)
        & (key_pos[None, :] >= 0)
    )
    scores = jnp.where(allowed[None], scores, -1e30)
    row_max = scores.max(-1, keepdims=True)
    numerators = jnp.exp(scores - row_max)
    probability = numerators / numerators.sum(-1, keepdims=True)
    weights = probability.astype(jnp.bfloat16)
    output = jnp.einsum(
        "hfe,ehd->fhd", weights, value_heads, preferred_element_type=jnp.float32
    ).reshape(row_count, model_width)
    d_out = (128.0 * (output - target.astype(jnp.float32))).astype(jnp.bfloat16)
    d_out = d_out.reshape(row_count, head_count, head_dim)
    grad_v = jnp.einsum("hfe,fhd->ehd", weights, d_out, preferred_element_type=jnp.float32)
    d_prob = jnp.einsum("fhd,ehd->hfe", d_out, value_heads, preferred_element_type=jnp.float32)
    row_inner = (probability * d_prob).sum(-1, keepdims=True)
    d_scores = (probability * (d_prob - row_inner) * factor).astype(jnp.bfloat16)
    grad_q = jnp.einsum("hfe,ehd->fhd", d_scores, key_heads, preferred_element_type=jnp.float32)
    grad_k = jnp.einsum("hfe,fhd->ehd", d_scores, query_heads, preferred_element_type=jnp.float32)
    return (
        grad_q.reshape(row_count, model_width),
        grad_k.reshape(ext_count, model_width),
        grad_v.reshape(ext_count, model_width),
    )


def local(queries, keys, values):
    row_count, model_width = queries.shape
    head_count = HEADS
    head_dim = model_width // head_count
    factor = head_dim ** (-0.5)
    query_heads = queries.reshape(row_count, head_count, head_dim)
    start_state = (
        jnp.full((head_count, row_count), -1e30, jnp.float32),
        jnp.zeros((head_count, row_count), jnp.float32),
        jnp.zeros((row_count, head_count, head_dim), jnp.float32),
    )
    absorb_key_piece = lax.all_gather(keys, "dev", axis=0, tiled=True)
    absorb_value_piece = lax.all_gather(values, "dev", axis=0, tiled=True)
    piece_rows = absorb_key_piece.shape[0]
    block_rows = 256
    key_blocks = absorb_key_piece.reshape(
        piece_rows // block_rows, block_rows, head_count, head_dim
    )
    value_blocks = absorb_value_piece.reshape(
        piece_rows // block_rows, block_rows, head_count, head_dim
    )

    def one_block(block_index, inner_state):
        run_max, run_total, run_acc = inner_state
        key_block = key_blocks[block_index]
        value_block = value_blocks[block_index]
        scores = (
            jnp.einsum("fhd,khd->hfk", query_heads, key_block, preferred_element_type=jnp.float32)
            * factor
        )
        new_max = jnp.maximum(run_max, scores.max(-1))
        old_scale = jnp.exp(run_max - new_max)
        numerators = jnp.exp(scores - new_max[..., None])
        new_total = run_total * old_scale + numerators.sum(-1)
        addend = jnp.einsum(
            "hfk,khd->fhd",
            numerators.astype(jnp.bfloat16),
            value_block,
            preferred_element_type=jnp.float32,
        )
        new_acc = run_acc * jnp.transpose(old_scale)[:, :, None] + addend
        return (new_max, new_total, new_acc)

    run_max, run_total, run_acc = lax.fori_loop(0, piece_rows // block_rows, one_block, start_state)
    target = (
        (run_acc / jnp.transpose(run_total)[:, :, None])
        .reshape(row_count, model_width)
        .astype(jnp.bfloat16)
    )
    reach_count = -(-WINDOW // row_count)
    halo_keys = []
    halo_values = []
    for back_step in range(reach_count, 0, -1):
        key_piece, value_piece = passed_along((keys, values), ("seg", "dev"), back_step)
        halo_keys.append(key_piece)
        halo_values.append(value_piece)
    ext_keys = jnp.concatenate([jnp.concatenate(halo_keys, 0), keys], 0)
    ext_values = jnp.concatenate([jnp.concatenate(halo_values, 0), values], 0)
    first_row = lax.axis_index(("seg", "dev")) * row_count
    grad_q, grad_k, grad_v = student_pass(
        queries, ext_keys, ext_values, target, first_row, head_count
    )
    pad_rows = reach_count * row_count - WINDOW
    zero_rows = jnp.zeros((pad_rows, model_width), jnp.bfloat16)
    halo_grad_k = jnp.concatenate([zero_rows, grad_k[:WINDOW].astype(jnp.bfloat16)], 0)
    halo_grad_v = jnp.concatenate([zero_rows, grad_v[:WINDOW].astype(jnp.bfloat16)], 0)
    local_k = grad_k[WINDOW:]
    local_v = grad_v[WINDOW:]
    for back_step in range(reach_count, 0, -1):
        offset_rows = (reach_count - back_step) * row_count
        piece_k = halo_grad_k[offset_rows : offset_rows + row_count]
        piece_v = halo_grad_v[offset_rows : offset_rows + row_count]
        back_k, back_v = passed_along((piece_k, piece_v), ("seg", "dev"), -back_step)
        local_k = local_k + back_k.astype(jnp.float32)
        local_v = local_v + back_v.astype(jnp.float32)
    return (grad_q.astype(jnp.bfloat16), local_k.astype(jnp.bfloat16), local_v.astype(jnp.bfloat16))


def solution(mesh):
    in_specs = (P(("seg", "dev"), None), P(("seg", "dev"), None), P(("seg", "dev"), None))
    out_specs = (P(("seg", "dev"), None), P(("seg", "dev"), None), P(("seg", "dev"), None))
    return jax.shard_map(local, mesh=mesh, in_specs=in_specs, out_specs=out_specs, check_vma=False)
```

profile of v0, /device:TPU:36, one launch (start us, length us, event | category | flops | bytes accessed | tf_op | source)
XLA Modules:
  0.0 665.9 jit_solution(2360740809766414248)
XLA Ops:
  8.6 3.1 collective-permute-start.1
  11.8 9.3 %collective-permute-start = (bf16[128,1536]{1,0:T(8,128)(2,1)}, bf16[128,1536]{1,0:T(8,128)(2,1)}, u32[]{:S(2)}, u32[]{:S(2)}) collective-permute-start(bf16[128,1536]{1,0:T(8,128)(2,1)} %param.6), channel_id=1, source_target_pairs={{0,2},{1,3},{2,4},{3,5},{4,6},{5,7},{6,8},{7,9},{8,10},{9,11},{10,... | collective-permute-start | bytes 1179656 | tf_op jit(solution)/shard_map/ppermute | solution.py:13
  21.1 4.0 collective-permute-start.3
  25.1 8.1 %collective-permute-start.2 = (bf16[128,1536]{1,0:T(8,128)(2,1)}, bf16[128,1536]{1,0:T(8,128)(2,1)}, u32[]{:S(2)}, u32[]{:S(2)}) collective-permute-start(bf16[128,1536]{1,0:T(8,128)(2,1)} %param.7), channel_id=1, source_target_pairs={{0,2},{1,3},{2,4},{3,5},{4,6},{5,7},{6,8},{7,9},{8,10},{9,11},{10,... | collective-permute-start | bytes 1179656 | tf_op jit(solution)/shard_map/ppermute | solution.py:13
  35.6 43.7 %collective-permute-done = bf16[128,1536]{1,0:T(8,128)(2,1)} collective-permute-done((bf16[128,1536]{1,0:T(8,128)(2,1)}, bf16[128,1536]{1,0:T(8,128)(2,1)}, u32[]{:S(2)}, u32[]{:S(2)}) %collective-permute-start) | collective-permute-done | bytes 393248 | tf_op jit(solution)/shard_map/ppermute | solution.py:13
  82.1 11.5 %collective-permute-done.2 = bf16[128,1536]{1,0:T(8,128)(2,1)} collective-permute-done((bf16[128,1536]{1,0:T(8,128)(2,1)}, bf16[128,1536]{1,0:T(8,128)(2,1)}, u32[]{:S(2)}, u32[]{:S(2)}) %collective-permute-start.2) | collective-permute-done | bytes 393248 | tf_op jit(solution)/shard_map/ppermute | solution.py:13
  96.1 4.2 fusion.55
  100.3 183.1 %all-gather.3.cloned.1.call-done = bf16[2048,1536]{1,0:T(8,128)(2,1)} async-done(((bf16[128,1536]{1,0:T(8,128)(2,1)}), bf16[2048,1536]{1,0:T(8,128)(2,1)}) %all-gather.3.cloned.1.call-update) | async-done | bytes 6291472 | tf_op jit(solution)/shard_map/all_gather | solution.py:70
  283.4 13.7 %reshape.136 = bf16[8,256,16,96]{3,2,1,0:T(8,128)(2,1)} reshape(bf16[2048,1536]{1,0:T(8,128)(2,1)} %all-gather.3.cloned.1.call-done) | data formatting | bytes 12582912 | tf_op jit(solution)/shard_map/reshape | solution.py:74
  297.1 11.8 %copy.30 = bf16[8,256,16,96]{1,3,2,0:T(8,128)(2,1)} copy(bf16[8,256,16,96]{3,2,1,0:T(8,128)(2,1)} %reshape.136) | data formatting | bytes 12582912
  308.8 111.1 %all-gather.5.cloned.1.call-done = bf16[2048,1536]{1,0:T(8,128)(2,1)} async-done(((bf16[128,1536]{1,0:T(8,128)(2,1)}), bf16[2048,1536]{1,0:T(8,128)(2,1)}) %all-gather.5.cloned.1.call-update) | async-done | bytes 6291472 | tf_op jit(solution)/shard_map/all_gather | solution.py:71
  419.9 13.7 %reshape.137 = bf16[8,256,16,96]{3,2,1,0:T(8,128)(2,1)} reshape(bf16[2048,1536]{1,0:T(8,128)(2,1)} %all-gather.5.cloned.1.call-done) | data formatting | bytes 12582912 | tf_op jit(solution)/shard_map/reshape | solution.py:77
  433.6 11.7 %copy.31 = bf16[8,256,16,96]{1,3,2,0:T(8,128)(2,1)} copy(bf16[8,256,16,96]{3,2,1,0:T(8,128)(2,1)} %reshape.137) | data formatting | bytes 12582912
  445.2 31.1 %while.18 = (s32[]{:T(128)}, f32[16,128]{1,0:T(8,128)S(1)}, f32[16,128]{1,0:T(8,128)S(1)}, f32[128,16,96]{0,2,1:T(8,128)S(1)}, bf16[8,256,16,96]{1,3,2,0:T(8,128...) while((s32[]{:T(128)}, f32[16,128]{1,0:T(8,128)S(1)}, ...), condition=%wide.region_5.6_spmd.clone, body=%wide.region_2.5_spmd.clone.sunk | while | flops 206123008 | bytes 9961593 | solution.py:102
  447.3 1.8 fusion.85
  455.1 1.8 fusion.85
  459.0 1.8 fusion.85
  466.7 1.8 fusion.85
  470.6 1.8 fusion.85
  474.5 1.8 fusion.85
  476.4 2.8 fusion.39
  479.2 2.3 fusion.60
  481.8 2.8 fusion.59
  484.6 7.6 %fusion.56 = (bf16[384,16,96]{0,2,1:T(8,128)(2,1)}, f32[384,16,96]{0,2,1:T(8,128)}) fusion(bf16[128,16,96]{0,2,1:T(8,128)(2,1)S(1)} %get-tuple-element.277, f32[16,128,384]{1,2,0:T(8,128)} %fusion.60, f32[16,128,384]{1,2,0:T(8,128)} %get-tuple-element.190, f32[16,128]{1,0:T(8,128)S(1)} %get-tuple-element.189), kind=kOutput, calls=%fused_computation.68 | convolution fusion | flops 157092224 | bytes 10231808 | tf_op jit(solution)/shard_map/hfe,fhd->ehd/dot_general | solution.py:51
  493.7 2.5 collective-permute-start.5
  496.4 52.0 %collective-permute-start.4 = (bf16[128,1536]{1,0:T(8,128)(2,1)S(1)}, bf16[128,1536]{1,0:T(8,128)(2,1)}, u32[]{:S(2)}, u32[]{:S(2)}) collective-permute-start(bf16[128,1536]{1,0:T(8,128)(2,1)S(1)} %copy.36), channel_id=1, source_target_pairs={{2,0},{3,1},{4,2},{5,3},{6,4},{7,5},{8,6},{9,7},{10,8},{11,9},{12,... | collective-permute-start | bytes 1179656 | tf_op jit(solution)/shard_map/ppermute | solution.py:13
  548.3 5.9 fusion.40
  558.7 1.9 collective-permute-start.7
  562.3 3.4 collective-permute-start.6
  565.7 2.0 add_convert_fusion.1
  568.7 88.5 %collective-permute-done.6 = bf16[128,1536]{1,0:T(8,128)(2,1)S(1)} collective-permute-done((bf16[128,1536]{1,0:T(8,128)(2,1)S(1)}, bf16[128,1536]{1,0:T(8,128)(2,1)S(1)}, u32[]{:S(2)}, u32[]{:S(2)}) %collective-permute-start.6) | collective-permute-done | bytes 393248 | tf_op jit(solution)/shard_map/ppermute | solution.py:13
  657.2 1.9 add_convert_fusion
  (84 shorter events, 37.9 us)
Async XLA Ops:
  7.2 276.2 %all-gather.3.cloned.1.call-start = ((), (), s32[]{:S(2)}) async-start(), calls=%async_computation | async-start | bytes 6684672 | tf_op jit(solution)/shard_map/all_gather | solution.py:70
  7.9 412.0 %all-gather.5.cloned.1.call-start = ((), (), s32[]{:S(2)}) async-start(), calls=%async_computation.1 | async-start | bytes 6684672 | tf_op jit(solution)/shard_map/all_gather | solution.py:71
  8.6 26.2 %collective-permute-start.1 = (bf16[128,1536]{1,0:T(8,128)(2,1)}, bf16[128,1536]{1,0:T(8,128)(2,1)S(1)}, u32[]{:S(2)}, u32[]{:S(2)}) collective-permute-start(bf16[128,1536]{1,0:T(8,128)(2,1)} %param.6), channel_id=1, source_target_pairs={{0,1},{1,2},{2,3},{3,4},{4,5},{5,6},{6,7},{7,8},{8,9},{9,10},{10,1... | collective-permute-start | bytes 1179656 | tf_op jit(solution)/shard_map/ppermute | solution.py:13
  11.8 67.6 %collective-permute-start = (bf16[128,1536]{1,0:T(8,128)(2,1)}, bf16[128,1536]{1,0:T(8,128)(2,1)}, u32[]{:S(2)}, u32[]{:S(2)}) collective-permute-start(bf16[128,1536]{1,0:T(8,128)(2,1)} %param.6), channel_id=1, source_target_pairs={{0,2},{1,3},{2,4},{3,5},{4,6},{5,7},{6,8},{7,9},{8,10},{9,11},{10,... | collective-permute-start | bytes 1179656 | tf_op jit(solution)/shard_map/ppermute | solution.py:13
  21.1 61.0 %collective-permute-start.3 = (bf16[128,1536]{1,0:T(8,128)(2,1)}, bf16[128,1536]{1,0:T(8,128)(2,1)S(1)}, u32[]{:S(2)}, u32[]{:S(2)}) collective-permute-start(bf16[128,1536]{1,0:T(8,128)(2,1)} %param.7), channel_id=1, source_target_pairs={{0,1},{1,2},{2,3},{3,4},{4,5},{5,6},{6,7},{7,8},{8,9},{9,10},{10,1... | collective-permute-start | bytes 1179656 | tf_op jit(solution)/shard_map/ppermute | solution.py:13
  25.1 68.5 %collective-permute-start.2 = (bf16[128,1536]{1,0:T(8,128)(2,1)}, bf16[128,1536]{1,0:T(8,128)(2,1)}, u32[]{:S(2)}, u32[]{:S(2)}) collective-permute-start(bf16[128,1536]{1,0:T(8,128)(2,1)} %param.7), channel_id=1, source_target_pairs={{0,2},{1,3},{2,4},{3,5},{4,6},{5,7},{6,8},{7,9},{8,10},{9,11},{10,... | collective-permute-start | bytes 1179656 | tf_op jit(solution)/shard_map/ppermute | solution.py:13
  34.8 58.8 %copy-start.1 = (bf16[128,1536]{1,0:T(8,128)(2,1)S(1)}, bf16[128,1536]{1,0:T(8,128)(2,1)}, u32[]{:S(2)}) copy-start(bf16[128,1536]{1,0:T(8,128)(2,1)} %param.7) | copy-start | bytes 1179652
  34.8 0.7 copy-start.3
  476.4 2.9 copy-start
  479.2 2.6 copy-start.4
  492.3 56.1 %copy-start.2 = (bf16[384,1536]{0,1:T(8,128)(2,1)S(1)}, bf16[384,1536]{0,1:T(8,128)(2,1)}, u32[]{:S(2)}) copy-start(bf16[384,1536]{0,1:T(8,128)(2,1)} %copy.24) | copy-start | bytes 3538948
  493.7 72.0 %collective-permute-start.5 = (bf16[128,1536]{1,0:T(8,128)(2,1)S(1)}, bf16[128,1536]{1,0:T(8,128)(2,1)}, u32[]{:S(2)}, u32[]{:S(2)}) collective-permute-start(bf16[128,1536]{1,0:T(8,128)(2,1)S(1)} %copy.38), channel_id=1, source_target_pairs={{1,0},{2,1},{3,2},{4,3},{5,4},{6,5},{7,6},{8,7},{9,8},{10,9},{11,1... | collective-permute-start | bytes 1179656 | tf_op jit(solution)/shard_map/ppermute | solution.py:13
  496.4 69.3 %collective-permute-start.4 = (bf16[128,1536]{1,0:T(8,128)(2,1)S(1)}, bf16[128,1536]{1,0:T(8,128)(2,1)}, u32[]{:S(2)}, u32[]{:S(2)}) collective-permute-start(bf16[128,1536]{1,0:T(8,128)(2,1)S(1)} %copy.36), channel_id=1, source_target_pairs={{2,0},{3,1},{4,2},{5,3},{6,4},{7,5},{8,6},{9,7},{10,8},{11,9},{12,... | collective-permute-start | bytes 1179656 | tf_op jit(solution)/shard_map/ppermute | solution.py:13
  558.7 10.0 %collective-permute-start.7 = (bf16[128,1536]{1,0:T(8,128)(2,1)}, bf16[128,1536]{1,0:T(8,128)(2,1)}, u32[]{:S(2)}, u32[]{:S(2)}) collective-permute-start(bf16[128,1536]{1,0:T(8,128)(2,1)} %copy.42), channel_id=1, source_target_pairs={{1,0},{2,1},{3,2},{4,3},{5,4},{6,5},{7,6},{8,7},{9,8},{10,9},{11,1... | collective-permute-start | bytes 1179656 | tf_op jit(solution)/shard_map/ppermute | solution.py:13
  562.3 94.9 %collective-permute-start.6 = (bf16[128,1536]{1,0:T(8,128)(2,1)S(1)}, bf16[128,1536]{1,0:T(8,128)(2,1)S(1)}, u32[]{:S(2)}, u32[]{:S(2)}) collective-permute-start(bf16[128,1536]{1,0:T(8,128)(2,1)S(1)} %copy.40), channel_id=1, source_target_pairs={{2,0},{3,1},{4,2},{5,3},{6,4},{7,5},{8,6},{9,7},{10,8},{11,9},{12,... | collective-permute-start | bytes 1179656 | tf_op jit(solution)/shard_map/ppermute | solution.py:13
Sparse Core Ops, SparseCore 0:
  11.0 272.3 all-gather.2
  286.4 133.4 all-gather.4
where the time goes:
time: 668 us; the launch traced here: 666 us
  waiting for transfers between devices  440 us (66%)
  starting transfers between devices  84.4 us (13%)
  local copies, waits for them, and re-layouts  63.8 us (10%)
  matrix products  53.1 us (8%)
  between operations  14.3 us (2%)
  other arithmetic  9.59 us (1%)
    all_gather x1, waiting for transfers between devices, local(): absorb_key_piece = lax.all_gather(keys, 'dev', axis=0, tiled=True)  183 us
    ppermute x8, waiting for transfers between devices, passed_along(): lax.ppermute(value, axis, [(source, source + steps) for source in range(i...  145 us
    all_gather x1, waiting for transfers between devices, local(): absorb_value_piece = lax.all_gather(values, 'dev', axis=0, tiled=True)  111 us
    ppermute x8, starting transfers between devices, passed_along(): lax.ppermute(value, axis, [(source, source + steps) for source in range(i...  84.3 us
    unnamed x14, local copies, waits for them, and re-layouts  26.7 us
    dot_general x8, matrix products, one_block(): jnp.einsum('hfk,khd->fhd', numerators.astype(jnp.bfloat16), value_block,...  14.5 us
    reshape x1, local copies, waits for them, and re-layouts, local(): absorb_key_piece.reshape(piece_rows // block_rows, block_rows, head_count...  13.7 us
    reshape x1, local copies, waits for them, and re-layouts, local(): absorb_value_piece.reshape(piece_rows // block_rows, block_rows, head_cou...  13.7 us
  transfers between devices with their start and end apart: 10, of which 6 were waited for; matrix products, arithmetic and copies ran while one was open for 8% of the time, Pallas kernels for 0%

commit v1 on v0

--- a/solution.py
+++ b/solution.py
@@ -68,7 +68,9 @@
         jnp.zeros((row_count, head_count, head_dim), jnp.float32),
     )
     absorb_key_piece = lax.all_gather(keys, "dev", axis=0, tiled=True)
-    absorb_value_piece = lax.all_gather(values, "dev", axis=0, tiled=True)
+    absorb_value_piece = jnp.concatenate(
+        lax.all_to_all(jnp.stack([values] * lax.axis_size("dev")), "dev", 0, 0), axis=0
+    )
     piece_rows = absorb_key_piece.shape[0]
     block_rows = 256
     key_blocks = absorb_key_piece.reshape(

time: 668 us -> 819 us (1.23)
  the two profiles are of different devices: /device:TPU:36 before, /device:TPU:269 now
where the time goes in v1:
time: 819 us; the launch traced here: 817 us
  waiting for transfers between devices  619 us (76%)
  local copies, waits for them, and re-layouts  67.7 us (8%)
  matrix products  53.7 us (7%)
  starting transfers between devices  52.4 us (6%)
  between operations  14.3 us (2%)
  other arithmetic  9.59 us (1%)
    ppermute x8, waiting for transfers between devices, passed_along(): lax.ppermute(value, axis, [(source, source + steps) for source in range(i...  345 us
    all_gather x1, waiting for transfers between devices, local(): absorb_key_piece = lax.all_gather(keys, 'dev', axis=0, tiled=True)  274 us
    ppermute x8, starting transfers between devices, passed_along(): lax.ppermute(value, axis, [(source, source + steps) for source in range(i...  38.3 us
    unnamed x19, local copies, waits for them, and re-layouts  22.1 us
  transfers between devices with their start and end apart: 10, of which 7 were waited for; matrix products, arithmetic and copies ran while one was open for 6% of the time, Pallas kernels for 0%

profile of v1, /device:TPU:269, one launch (start us, length us, event | category | flops | bytes accessed | tf_op | source)
XLA Modules:
  0.0 817.1 jit_solution(18053480699231254651)
XLA Ops:
  8.4 3.8 stack.2
  12.2 14.0 %all-to-all-start = ((bf16[16,128,1536]{1,2,0:T(8,128)(2,1)}), bf16[16,128,1536]{1,2,0:T(8,128)(2,1)}, u32[]{:S(2)}, u32[]{:S(2)}) async-start(bf16[16,128,1536]{1,2,0:T(8,128)(2,1)} %stack.2), calls=%async_computation | async-start | bytes 12582912 | tf_op jit(solution)/shard_map/all_to_all | solution.py:72
  26.9 2.8 collective-permute-start.1
  29.7 2.5 collective-permute-start
  32.2 3.7 collective-permute-start.3
  36.0 3.9 collective-permute-start.2
  40.4 23.0 %collective-permute-done.1 = bf16[128,1536]{1,0:T(8,128)(2,1)S(1)} collective-permute-done((bf16[128,1536]{1,0:T(8,128)(2,1)S(1)}, bf16[128,1536]{1,0:T(8,128)(2,1)S(1)}, u32[]{:S(2)}, u32[]{:S(2)}) %collective-permute-start.1) | collective-permute-done | bytes 393248 | tf_op jit(solution)/shard_map/ppermute | solution.py:13
  64.1 137.6 %collective-permute-done = bf16[128,1536]{1,0:T(8,128)(2,1)} collective-permute-done((bf16[128,1536]{1,0:T(8,128)(2,1)S(1)}, bf16[128,1536]{1,0:T(8,128)(2,1)}, u32[]{:S(2)}, u32[]{:S(2)}) %collective-permute-start) | collective-permute-done | bytes 393248 | tf_op jit(solution)/shard_map/ppermute | solution.py:13
  204.3 16.5 %collective-permute-done.2 = bf16[128,1536]{1,0:T(8,128)(2,1)} collective-permute-done((bf16[128,1536]{1,0:T(8,128)(2,1)S(1)}, bf16[128,1536]{1,0:T(8,128)(2,1)}, u32[]{:S(2)}, u32[]{:S(2)}) %collective-permute-start.2) | collective-permute-done | bytes 393248 | tf_op jit(solution)/shard_map/ppermute | solution.py:13
  223.5 4.3 fusion.55
  227.8 273.6 %all-gather.2.cloned.1.call-done = bf16[2048,1536]{1,0:T(8,128)(2,1)} async-done(((bf16[128,1536]{1,0:T(8,128)(2,1)}), bf16[2048,1536]{1,0:T(8,128)(2,1)}) %all-gather.2.cloned.1.call-update) | async-done | bytes 6291472 | tf_op jit(solution)/shard_map/all_gather | solution.py:70
  501.4 13.7 %reshape.134 = bf16[8,256,16,96]{3,2,1,0:T(8,128)(2,1)} reshape(bf16[2048,1536]{1,0:T(8,128)(2,1)} %all-gather.2.cloned.1.call-done) | data formatting | bytes 12582912 | tf_op jit(solution)/shard_map/reshape | solution.py:76
  515.0 11.7 %copy.52 = bf16[8,256,16,96]{1,3,2,0:T(8,128)(2,1)} copy(bf16[8,256,16,96]{3,2,1,0:T(8,128)(2,1)} %reshape.134) | data formatting | bytes 12582912
  526.8 8.5 %copy.51 = bf16[16,128,1536]{1,0,2:T(8,128)(2,1)} copy(bf16[16,128,1536]{1,2,0:T(8,128)(2,1)} %all-to-all-done) | data formatting | bytes 12582912 | tf_op jit(solution)/shard_map/all_to_all | solution.py:72
  535.3 10.0 %reshape_reshape.3 = bf16[8,256,16,96]{1,0,3,2:T(8,128)(2,1)} reshape(bf16[16,128,1536]{1,0,2:T(8,128)(2,1)} %copy.51) | data formatting | bytes 12582912 | tf_op jit(solution)/shard_map/reshape;reshape | solution.py:79
  545.3 7.0 copy.53
  552.2 31.1 %while.18 = (s32[]{:T(128)}, f32[16,128]{1,0:T(8,128)S(1)}, f32[16,128]{1,0:T(8,128)S(1)}, f32[128,16,96]{0,2,1:T(8,128)S(1)}, bf16[8,256,16,96]{1,3,2,0:T(8,128...) while((s32[]{:T(128)}, f32[16,128]{1,0:T(8,128)S(1)}, ...), condition=%wide.region_5.6_spmd.clone, body=%wide.region_2.5_spmd.clone.sunk | while | flops 206123008 | bytes 9961593 | solution.py:104
  562.1 1.8 fusion.85
  583.4 2.8 fusion.39
  586.2 2.3 fusion.60
  588.8 2.8 fusion.59
  591.6 7.9 fusion.56
  600.9 1.9 collective-permute-start.5
  603.0 19.7 %collective-permute-start.4 = (bf16[128,1536]{1,0:T(8,128)(2,1)S(1)}, bf16[128,1536]{1,0:T(8,128)(2,1)}, u32[]{:S(2)}, u32[]{:S(2)}) collective-permute-start(bf16[128,1536]{1,0:T(8,128)(2,1)S(1)} %copy.58), channel_id=1, source_target_pairs={{2,0},{3,1},{4,2},{5,3},{6,4},{7,5},{8,6},{9,7},{10,8},{11,9},{12,... | collective-permute-start | bytes 1179656 | tf_op jit(solution)/shard_map/ppermute | solution.py:13
  622.8 6.1 fusion.40
  633.4 1.9 collective-permute-start.7
  637.0 1.9 collective-permute-start.6
  638.9 41.6 %collective-permute-done.5 = bf16[128,1536]{1,0:T(8,128)(2,1)} collective-permute-done((bf16[128,1536]{1,0:T(8,128)(2,1)S(1)}, bf16[128,1536]{1,0:T(8,128)(2,1)}, u32[]{:S(2)}, u32[]{:S(2)}) %collective-permute-start.5) | collective-permute-done | bytes 393248 | tf_op jit(solution)/shard_map/ppermute | solution.py:13
  680.5 111.1 %collective-permute-done.4 = bf16[128,1536]{1,0:T(8,128)(2,1)} collective-permute-done((bf16[128,1536]{1,0:T(8,128)(2,1)S(1)}, bf16[128,1536]{1,0:T(8,128)(2,1)}, u32[]{:S(2)}, u32[]{:S(2)}) %collective-permute-start.4) | collective-permute-done | bytes 393248 | tf_op jit(solution)/shard_map/ppermute | solution.py:13
  791.6 2.0 add_convert_fusion.1
  793.6 14.8 %collective-permute-done.6 = bf16[128,1536]{1,0:T(8,128)(2,1)S(1)} collective-permute-done((bf16[128,1536]{1,0:T(8,128)(2,1)S(1)}, bf16[128,1536]{1,0:T(8,128)(2,1)S(1)}, u32[]{:S(2)}, u32[]{:S(2)}) %collective-permute-start.6) | collective-permute-done | bytes 393248 | tf_op jit(solution)/shard_map/ppermute | solution.py:13
  808.4 1.9 add_convert_fusion
  (90 shorter events, 45.3 us)
Async XLA Ops:
  12.2 14.7 %copy-start.2 = (bf16[128,1536]{1,0:T(8,128)(2,1)S(1)}, bf16[128,1536]{1,0:T(8,128)(2,1)}, u32[]{:S(2)}) copy-start(bf16[128,1536]{1,0:T(8,128)(2,1)} %param.6) | copy-start | bytes 1179652
  12.2 20.1 %copy-start.1 = (bf16[128,1536]{1,0:T(8,128)(2,1)S(1)}, bf16[128,1536]{1,0:T(8,128)(2,1)}, u32[]{:S(2)}) copy-start(bf16[128,1536]{1,0:T(8,128)(2,1)} %param.7) | copy-start | bytes 1179652
  12.2 27.7 %copy-start.5 = (bf16[128,1536]{1,0:T(8,128)(2,1)S(1)}, bf16[128,1536]{1,0:T(8,128)(2,1)}, u32[]{:S(2)}) copy-start(bf16[128,1536]{1,0:T(8,128)(2,1)} %param.5) | copy-start | bytes 1179652
  12.2 514.6 %all-to-all-start = ((bf16[16,128,1536]{1,2,0:T(8,128)(2,1)}), bf16[16,128,1536]{1,2,0:T(8,128)(2,1)}, u32[]{:S(2)}, u32[]{:S(2)}) async-start(bf16[16,128,1536]{1,2,0:T(8,128)(2,1)} %stack.2), calls=%async_computation | async-start | bytes 12582912 | tf_op jit(solution)/shard_map/all_to_all | solution.py:72
  26.2 475.2 %all-gather.2.cloned.1.call-start = ((), (), s32[]{:S(2)}) async-start(), calls=%async_computation.1 | async-start | bytes 6684672 | tf_op jit(solution)/shard_map/all_gather | solution.py:70
  26.9 36.4 %collective-permute-start.1 = (bf16[128,1536]{1,0:T(8,128)(2,1)S(1)}, bf16[128,1536]{1,0:T(8,128)(2,1)S(1)}, u32[]{:S(2)}, u32[]{:S(2)}) collective-permute-start(bf16[128,1536]{1,0:T(8,128)(2,1)S(1)} %copy-done.2), channel_id=1, source_target_pairs={{0,1},{1,2},{2,3},{3,4},{4,5},{5,6},{6,7},{7,8},{8,9},{9,10},{10,1... | collective-permute-start | bytes 1179656 | tf_op jit(solution)/shard_map/ppermute | solution.py:13
  29.7 172.0 %collective-permute-start = (bf16[128,1536]{1,0:T(8,128)(2,1)S(1)}, bf16[128,1536]{1,0:T(8,128)(2,1)}, u32[]{:S(2)}, u32[]{:S(2)}) collective-permute-start(bf16[128,1536]{1,0:T(8,128)(2,1)S(1)} %copy-done.2), channel_id=1, source_target_pairs={{0,2},{1,3},{2,4},{3,5},{4,6},{5,7},{6,8},{7,9},{8,10},{9,11},{10,... | collective-permute-start | bytes 1179656 | tf_op jit(solution)/shard_map/ppermute | solution.py:13
  32.2 172.1 %collective-permute-start.3 = (bf16[128,1536]{1,0:T(8,128)(2,1)S(1)}, bf16[128,1536]{1,0:T(8,128)(2,1)}, u32[]{:S(2)}, u32[]{:S(2)}) collective-permute-start(bf16[128,1536]{1,0:T(8,128)(2,1)S(1)} %copy-done.1), channel_id=1, source_target_pairs={{0,1},{1,2},{2,3},{3,4},{4,5},{5,6},{6,7},{7,8},{8,9},{9,10},{10,1... | collective-permute-start | bytes 1179656 | tf_op jit(solution)/shard_map/ppermute | solution.py:13
  36.0 184.9 %collective-permute-start.2 = (bf16[128,1536]{1,0:T(8,128)(2,1)S(1)}, bf16[128,1536]{1,0:T(8,128)(2,1)}, u32[]{:S(2)}, u32[]{:S(2)}) collective-permute-start(bf16[128,1536]{1,0:T(8,128)(2,1)S(1)} %copy-done.1), channel_id=1, source_target_pairs={{0,2},{1,3},{2,4},{3,5},{4,6},{5,7},{6,8},{7,9},{8,10},{9,11},{10,... | collective-permute-start | bytes 1179656 | tf_op jit(solution)/shard_map/ppermute | solution.py:13
  63.3 0.7 copy-start.4
  583.4 2.9 copy-start
  586.2 2.6 copy-start.6
  599.5 23.3 %copy-start.3 = (bf16[384,1536]{0,1:T(8,128)(2,1)S(1)}, bf16[384,1536]{0,1:T(8,128)(2,1)}, u32[]{:S(2)}) copy-start(bf16[384,1536]{0,1:T(8,128)(2,1)} %copy.45) | copy-start | bytes 3538948
  600.9 79.6 %collective-permute-start.5 = (bf16[128,1536]{1,0:T(8,128)(2,1)S(1)}, bf16[128,1536]{1,0:T(8,128)(2,1)}, u32[]{:S(2)}, u32[]{:S(2)}) collective-permute-start(bf16[128,1536]{1,0:T(8,128)(2,1)S(1)} %copy.60), channel_id=1, source_target_pairs={{1,0},{2,1},{3,2},{4,3},{5,4},{6,5},{7,6},{8,7},{9,8},{10,9},{11,1... | collective-permute-start | bytes 1179656 | tf_op jit(solution)/shard_map/ppermute | solution.py:13
  603.0 188.6 %collective-permute-start.4 = (bf16[128,1536]{1,0:T(8,128)(2,1)S(1)}, bf16[128,1536]{1,0:T(8,128)(2,1)}, u32[]{:S(2)}, u32[]{:S(2)}) collective-permute-start(bf16[128,1536]{1,0:T(8,128)(2,1)S(1)} %copy.58), channel_id=1, source_target_pairs={{2,0},{3,1},{4,2},{5,3},{6,4},{7,5},{8,6},{9,7},{10,8},{11,9},{12,... | collective-permute-start | bytes 1179656 | tf_op jit(solution)/shard_map/ppermute | solution.py:13
  633.4 160.2 %collective-permute-start.7 = (bf16[128,1536]{1,0:T(8,128)(2,1)}, bf16[128,1536]{1,0:T(8,128)(2,1)}, u32[]{:S(2)}, u32[]{:S(2)}) collective-permute-start(bf16[128,1536]{1,0:T(8,128)(2,1)} %copy.64), channel_id=1, source_target_pairs={{1,0},{2,1},{3,2},{4,3},{5,4},{6,5},{7,6},{8,7},{9,8},{10,9},{11,1... | collective-permute-start | bytes 1179656 | tf_op jit(solution)/shard_map/ppermute | solution.py:13
  637.0 171.4 %collective-permute-start.6 = (bf16[128,1536]{1,0:T(8,128)(2,1)S(1)}, bf16[128,1536]{1,0:T(8,128)(2,1)S(1)}, u32[]{:S(2)}, u32[]{:S(2)}) collective-permute-start(bf16[128,1536]{1,0:T(8,128)(2,1)S(1)} %copy.62), channel_id=1, source_target_pairs={{2,0},{3,1},{4,2},{5,3},{6,4},{7,5},{8,6},{9,7},{10,8},{11,9},{12,... | collective-permute-start | bytes 1179656 | tf_op jit(solution)/shard_map/ppermute | solution.py:13
Sparse Core Ops, SparseCore 0:
  30.0 471.2 all-gather.1
